TPU v7x, 256 devices: a whole 4x4x8 slice. The times are simulated.
256 devices in a mesh: gx: 16 (over z, core), gy: 16 (over x, y).
Axes of the slice: x: 4, y: 4, z: 8, core: 2. Of those that a mesh axis runs over, the one named last changes fastest.
Arguments:
- positions: float32 [16, 16, 3, 256], P('gx', 'gy'), may hold values from 0 to 10
- species: int32 [16, 16, 256], P('gx', 'gy'), may hold values from 0 to 5
- neighbours: int32 [16, 16, 256, 12], P('gx', 'gy'), may hold values from 0 to 2303
- counts: int32 [16, 16, 256], P('gx', 'gy'), may hold values from 6 to 12
- species_embed: float32 [6, 128], replicated, may hold values from -6 to 6
- radial: float32 [2, 2, 8, 128], replicated, may hold values from -2 to 2
- mixing: float32 [2, 2, 128, 128], replicated, may hold values from -0.5 to 0.5
- read_hidden: float32 [128, 128], replicated, may hold values from -0.5 to 0.5
- read_out: float32 [128], replicated, may hold values from -0.5 to 0.5
- charge_map: float32 [128, 64], replicated, may hold values from -0.5 to 0.5
- wavevectors: int32 [3, 4096], replicated, may hold values from -8 to 8, as said below
Outputs:
- forces: float32 [16, 16, 3, 256], P('gx', 'gy')
- site_energy: float32 [16, 16, 256], P('gx', 'gy')
Inputs may be any that keep to these rules, and one draw needn't show every extreme that they name: `neighbours`: entry (3 a + b) * 256 + t names atom t of the cell offset by (a - 1, b - 1) along gx, gy, periodically. Slots n < counts are used. `wavevectors`: the 4096 triples are distinct, and no triple has its first two components both zero.
All inputs are finite; a program needn't handle non-finite values.
Results may differ from a plain program's by a relative error of at most 0.0017.
Values may be sent and summed in bfloat16 or wider, within the bound.
A program may use at most 128 MiB of HBM per device.

v0:
```python
import math
import jax
import jax.numpy as jnp
from jax import lax
from jax.sharding import PartitionSpec as P

cell_width = 10.0
box_height = 30.0
cut_radius = 50.0
soften = 0.25
screen = 0.5
smear_width = 0.5
highest = lax.Precision.HIGHEST


def passed_along(block, axis, distance):
    devices = range(lax.axis_size(axis))
    route = [((i - distance) % len(devices), i) for i in devices]
    return lax.ppermute(block, axis, route)


def with_halo(block, sides, width):
    for axis, dim in sides:
        count = lax.axis_size(axis)
        forward = [(i, i + 1) for i in range(count - 1)]
        forward.append((count - 1, 0))
        backward = [(target, source) for source, target in forward]
        low = lax.ppermute(
            lax.slice_in_dim(block, block.shape[dim] - width, None, axis=dim), axis, forward
        )
        high = lax.ppermute(lax.slice_in_dim(block, 0, width, axis=dim), axis, backward)
        block = jnp.concatenate([low, block, high], axis=dim)
    return block


def build_frame(extended):
    offsets = (jnp.arange(3, dtype=jnp.float32) - 1.0) * cell_width
    shift_x = jnp.broadcast_to(offsets[:, None], (3, 3))
    shift_y = jnp.broadcast_to(offsets[None, :], (3, 3))
    shifts = jnp.stack([shift_x, shift_y, jnp.zeros((3, 3), jnp.float32)], axis=2)
    coords = extended[:, :, :3, :] + shifts[:, :, :, None]
    src_pos = jnp.moveaxis(coords, 2, 0).reshape(3, -1)
    kind_codes = extended[:, :, 3, :].reshape(-1)
    return (src_pos, kind_codes)


def embed_rows(kind_codes, species_embed):
    lookup = (
        kind_codes[:, None] == jnp.arange(species_embed.shape[0], dtype=jnp.float32)[None, :]
    ).astype(jnp.float32)
    return jnp.dot(lookup, species_embed, precision=highest)


def interact(h_dst, h_src, own_pos, src_pos, neighbour_ids, slot_counts, radial_pair, mix_pair):
    slots = neighbour_ids.shape[1]
    orders = radial_pair.shape[1]
    relative = src_pos[:, neighbour_ids] - own_pos[:, :, None]
    distance = jnp.sqrt(jnp.sum(relative * relative, axis=0) + soften)
    unit_vec = relative / distance[None]
    frequency = jnp.arange(1, orders + 1, dtype=jnp.float32) * (math.pi / cut_radius)
    arg_scaled = distance[:, :, None] * frequency
    radial_basis = jnp.sin(arg_scaled) / arg_scaled
    live_slots = (jnp.arange(slots)[None, :] < slot_counts[:, None]).astype(jnp.float32)
    weight_zero = (
        jnp.einsum("anr,rc->anc", radial_basis, radial_pair[0], precision=highest)
        * live_slots[:, :, None]
    )
    weight_one = (
        jnp.einsum("anr,rc->anc", radial_basis, radial_pair[1], precision=highest)
        * live_slots[:, :, None]
    )
    source = h_src[neighbour_ids]
    norm_factor = 1.0 / math.sqrt(slots)
    msg_zero = jnp.sum(weight_zero * source, axis=1) * norm_factor
    msg_one = (
        jnp.einsum("anc,xan->xac", weight_one * source, unit_vec, precision=highest) * norm_factor
    )
    squares = jnp.sum(msg_one * msg_one, axis=0)
    preact = jnp.dot(msg_zero, mix_pair[0], precision=highest) + jnp.dot(
        squares, mix_pair[1], precision=highest
    )
    return h_dst + jax.nn.silu(preact)


def first_layer(own_pos, src_pos, initial_src, neighbour_ids, slot_counts, radial, mixing):
    atom_count = own_pos.shape[1]
    return interact(
        initial_src[4 * atom_count : 5 * atom_count],
        initial_src,
        own_pos,
        src_pos,
        neighbour_ids,
        slot_counts,
        radial[0],
        mixing[0],
    )


def second_section(
    hidden_src,
    own_pos,
    src_pos,
    neighbour_ids,
    slot_counts,
    radial,
    mixing,
    read_hidden,
    read_out,
    charge_map,
):
    atom_count = own_pos.shape[1]
    hidden_two = interact(
        hidden_src[4 * atom_count : 5 * atom_count],
        hidden_src,
        own_pos,
        src_pos,
        neighbour_ids,
        slot_counts,
        radial[1],
        mixing[1],
    )
    energy = jnp.dot(
        jax.nn.silu(jnp.dot(hidden_two, read_hidden, precision=highest)),
        read_out,
        precision=highest,
    )
    charges = jnp.dot(hidden_two, charge_map, precision=highest)
    return (energy, charges)


def wave_terms(wavevectors, grid_x, grid_y):
    lengths = jnp.array([grid_x * cell_width, grid_y * cell_width, box_height], dtype=jnp.float32)
    wave_phys = 2.0 * math.pi * wavevectors.astype(jnp.float32) / lengths[:, None]
    wave_sq = jnp.sum(wave_phys * wave_phys, axis=0)
    green_weight = jnp.exp(-smear_width * wave_sq) / (wave_sq + screen * screen)
    return (wave_phys, green_weight)


def phase_pair(global_pos, wave_part):
    angle = (
        global_pos[0][:, None] * wave_part[0][None, :]
        + global_pos[1][:, None] * wave_part[1][None, :]
        + global_pos[2][:, None] * wave_part[2][None, :]
    )
    return (jnp.cos(angle), jnp.sin(angle))


def structure_term(charges, global_pos, wave_part):
    cosine, sine_part = phase_pair(global_pos, wave_part)
    dims = (((0,), (0,)), ((), ()))
    real_part = lax.dot_general(cosine, charges, dims, precision=highest)
    imag_part = lax.dot_general(sine_part, charges, dims, precision=highest)
    return jnp.concatenate([real_part, imag_part], axis=1)


def fold_terms(carried, piece_rows, start_row, charges, global_pos, wave_phys):
    potential, lr_grad = carried
    row_count = piece_rows.shape[0]
    lat_width = charges.shape[1]
    wave_part = lax.dynamic_slice_in_dim(
        wave_phys, jnp.asarray(start_row).astype(jnp.int32), row_count, 1
    )
    cosine, sine_part = phase_pair(global_pos, wave_part)
    weight_re = piece_rows[:, :lat_width]
    weight_im = piece_rows[:, lat_width:]
    potential = (
        potential
        + jnp.dot(cosine, weight_re, precision=highest)
        + jnp.dot(sine_part, weight_im, precision=highest)
    )
    dims = (((1,), (1,)), ((), ()))
    proj_re = lax.dot_general(charges, weight_re, dims, precision=highest)
    proj_im = lax.dot_general(charges, weight_im, dims, precision=highest)
    phase_turn = cosine * proj_im - sine_part * proj_re
    lr_grad = lr_grad + lax.dot_general(wave_part, phase_turn, dims, precision=highest)
    return (potential, lr_grad)


def send_back(cotangent_grid):
    column = cotangent_grid[:, 1]
    for shift_by, column_pick in ((1, 2), (-1, 0)):
        column = column + passed_along(cotangent_grid[:, column_pick], "gy", shift_by)
    running = column[1]
    for shift_by, column_pick in ((1, 2), (-1, 0)):
        running = running + passed_along(column[column_pick], "gx", shift_by)
    return running


def per_device(
    positions,
    species,
    neighbours,
    counts,
    species_embed,
    radial,
    mixing,
    read_hidden,
    read_out,
    charge_map,
    wavevectors,
):
    atom_count = positions.shape[3]
    width = read_hidden.shape[0]
    lat_width = charge_map.shape[1]
    wave_count = wavevectors.shape[1]
    own_pos = positions[0, 0]
    neighbour_ids = neighbours[0, 0]
    slot_counts = counts[0, 0]
    packed = jnp.concatenate([positions, species.astype(jnp.float32)[:, :, None, :]], axis=2)
    extended = with_halo(packed, (("gx", 0), ("gy", 1)), 1)
    src_pos, kind_codes = build_frame(extended)
    initial_src = embed_rows(kind_codes, species_embed)

    def layer_one(own_coords, source_coords):
        return first_layer(
            own_coords, source_coords, initial_src, neighbour_ids, slot_counts, radial, mixing
        )

    hidden_one, pull_one = jax.vjp(layer_one, own_pos, src_pos)
    hidden_low = hidden_one.astype(jnp.bfloat16)
    ghost_hidden = with_halo(hidden_low[None, None], (("gx", 0), ("gy", 1)), 1)
    hidden_src = ghost_hidden.reshape(9 * atom_count, width).astype(jnp.float32)

    def section_two(source_hidden, own_coords, source_coords):
        return second_section(
            source_hidden,
            own_coords,
            source_coords,
            neighbour_ids,
            slot_counts,
            radial,
            mixing,
            read_hidden,
            read_out,
            charge_map,
        )

    (energy_sr, charges), pull_two = jax.vjp(section_two, hidden_src, own_pos, src_pos)
    grid_x = lax.axis_size("gx")
    grid_y = lax.axis_size("gy")
    row_index = lax.axis_index("gx")
    col_index = lax.axis_index("gy")
    anchor = jnp.stack(
        [
            row_index.astype(jnp.float32) * cell_width,
            col_index.astype(jnp.float32) * cell_width,
            jnp.zeros((), jnp.float32),
        ]
    )
    global_pos = own_pos + anchor[:, None]
    wave_phys, green_weight = wave_terms(wavevectors, grid_x, grid_y)
    start_state = (
        jnp.zeros((atom_count, lat_width), jnp.float32),
        jnp.zeros((3, atom_count), jnp.float32),
    )

    def fold_piece(carried, piece_rows, start_row):
        return fold_terms(carried, piece_rows, start_row, charges, global_pos, wave_phys)

    block_rows = math.gcd(wave_count, 512)
    block_total = wave_count // block_rows

    def term_block(block_idx):
        return structure_term(
            charges,
            global_pos,
            lax.dynamic_slice_in_dim(wave_phys, block_idx * block_rows, block_rows, 1),
        )

    partial_sf = lax.map(term_block, jnp.arange(block_total)).reshape(wave_count, 2 * lat_width)
    structure = lax.psum(partial_sf, ("gx", "gy"))
    weighted = green_weight[:, None] * structure

    def fold_block(block_idx, carried):
        start_row = block_idx * block_rows
        return fold_piece(
            carried, lax.dynamic_slice_in_dim(weighted, start_row, block_rows, 0), start_row
        )

    potential, lr_grad = lax.fori_loop(0, block_total, fold_block, start_state)
    lr_scale = 1.0 / math.sqrt(wave_count * lat_width * atom_count * grid_x * grid_y)
    site_energy = energy_sr + lr_scale * jnp.sum(charges * potential, axis=1)
    grad_hidden, grad_own_two, grad_src_two = pull_two(
        (jnp.ones_like(energy_sr), 2.0 * lr_scale * potential)
    )
    grad_hidden_own = send_back(grad_hidden.reshape(3, 3, atom_count, width))
    grad_own_one, grad_src_one = pull_one(grad_hidden_own)
    grad_src = jnp.moveaxis((grad_src_one + grad_src_two).reshape(3, 3, 3, atom_count), 0, 2)
    grad_back = send_back(grad_src)
    forces = -(grad_own_one + grad_own_two + grad_back + 2.0 * lr_scale * lr_grad)
    return (forces[None, None], site_energy[None, None])


def solution(mesh):
    in_specs = (
        P("gx", "gy", None, None),
        P("gx", "gy", None),
        P("gx", "gy", None, None),
        P("gx", "gy", None),
        P(),
        P(),
        P(),
        P(),
        P(),
        P(),
        P(),
    )
    out_specs = (P("gx", "gy", None, None), P("gx", "gy", None))
    return jax.shard_map(
        per_device, mesh=mesh, in_specs=in_specs, out_specs=out_specs, check_vma=False
    )
```

profile of v0, /device:TPU:127, one launch (start us, length us, event | category | flops | bytes accessed | tf_op | source)
XLA Modules:
  0.0 658.0 jit_solution(15282596504475978514)
XLA Ops:
  17.3 4.3 collective-permute-start.2
  24.4 8.1 %gather_fusion = f32[3072,3]{1,0:T(8,128)S(1)} fusion(f32[3,2304]{0,1:T(8,128)S(1)} %bitcast.271, s32[3072]{0:T(1024)S(1)} %broadcast_clamp_fusion), kind=kCustom, calls=%fused_computation | custom fusion | bytes 86016 | tf_op jit(solution)/shard_map/jvp()/gather | solution.py:57
  36.6 10.8 %gather_fusion.1 = f32[3072,128]{1,0:T(8,128)} fusion(f32[2304,128]{1,0:T(8,128)S(1)} %fusion.133, s32[3072]{0:T(1024)S(1)} %broadcast_clamp_fusion), kind=kCustom, calls=%fused_computation.1 | custom fusion | bytes 3158016 | tf_op jit(solution)/shard_map/jvp()/gather | solution.py:72
  49.1 4.2 multiply_reduce_fusion.1
  53.3 4.4 multiply_multiply_fusion
  58.0 4.0 multiply_reduce_fusion.3
  67.3 5.2 collective-permute-start.6
  72.5 5.0 convolution_multiply_fusion.1
  77.7 10.8 %gather_fusion.2 = f32[3072,128]{1,0:T(8,128)} fusion(f32[2304,128]{1,0:T(8,128)S(1)} %bitcast_convert_fusion, s32[3072]{0:T(1024)S(1)} %broadcast_clamp_fusion), kind=kCustom, calls=%fused_computation.2 | custom fusion | bytes 3158016 | tf_op jit(solution)/shard_map/jvp()/gather | solution.py:72
  90.0 6.9 %copy_multiply_fusion.1 = (f32[256,12,128]{2,0,1:T(8,128)S(1)}, f32[256,128]{1,0:T(8,128)S(1)}, f32[256,12,128]{2,0,1:T(8,128)}) fusion(f32[256,12,128]{2,1,0:T(8,128)S(1)} %reshape.168, f32[256,12,128]{2,0,1:T(8,128)} %convolution_multiply_fusion.1, f32[256,12]{0,1:T(8,128)S(1)} %fusion.161, f32[2,2,8,128]{3,2,1,0:T(8,128)} %param.21, ...), kind=kOutput, calls=%fused_computation.121 | convolution fusion | flops 39337984 | bytes 6451232 | tf_op jit(solution)/shard_map/jvp(anr,rc->anc)/dot_general | solution.py:69
  97.2 3.9 multiply_reduce_fusion.2
  102.4 62.1 %while.26 = (s32[]{:T(128)}, f32[8,512,128]{2,1,0:T(8,128)}, f32[3,256]{1,0:T(4,128)S(1)}, s32[8]{0:T(128)S(1)}, f32[3,4096]{1,0:T(4,128)}, /*index=5*/f32[256,6...) while((s32[]{:T(128)}, f32[8,512,128]{2,1,0:T(8,128)}, ...), condition=%wide.region_7.8_spmd, body=%wide.region_6.7_spmd.sunk | while | flops 202702848 | bytes 2003167 | solution.py:270
  166.3 260.0 %all-reduce.3.cloned.1.call-done = f32[4096,128]{1,0:T(8,128)} async-done(((f32[4096,128]{1,0:T(8,128)}), f32[4096,128]{1,0:T(8,128)}) %all-reduce.3.cloned.1.call-update) | async-done | bytes 2097168 | tf_op jit(solution)/shard_map/psum | solution.py:271
  428.5 87.4 %while.27 = (s32[]{:T(128)}, f32[256,64]{0,1:T(8,128)S(1)}, f32[3,256]{1,0:T(4,128)S(1)}, f32[3,256]{1,0:T(4,128)S(1)}, f32[3,4096]{1,0:T(4,128)}, /*index=5*/f3...) while((s32[]{:T(128)}, f32[256,64]{0,1:T(8,128)S(1)}, ...), condition=%wide.region_10.11_spmd.clone, body=%wide.region_9.10_spmd.clone.sunk | while | flops 410437120 | bytes 3739922 | solution.py:280
  518.0 4.0 fusion.88
  527.2 17.4 %scatter_fusion = f32[2304,128]{1,0:T(8,128)S(1)} fusion(f32[2304,128]{1,0:T(8,128)S(1)} %pad.3, s32[3072]{0:T(1024)S(1)} %reshape.153, f32[3072,128]{1,0:T(8,128)S(1)} %reshape.179), kind=kCustom, calls=%fused_computation.3 | custom fusion | flops 393216 | bytes 4730880 | tf_op jit(solution)/shard_map/transpose(jvp())/scatter-add | solution.py:72
  550.7 4.7 collective-permute-done.8
  555.4 3.8 collective-permute-done.9
  568.0 4.1 fusion.47
  572.1 5.3 fusion.89
  577.4 6.2 fusion.80
  586.8 3.9 fusion.52
  598.4 17.2 %scatter_custom_fusion.1 = f32[3,2304]{0,1:T(8,128)S(1)} fusion(s32[3072]{0:T(1024)S(1)} %reshape.153, f32[3072,3]{1,0:T(8,128)S(1)} %copy.264, f32[]{:T(128)} %constant.47.clone.1), kind=kCustom, calls=%fused_computation.107 | custom fusion | flops 9216 | bytes 27652 | tf_op jit(solution)/shard_map/transpose(jvp())/scatter-add | solution.py:57
  617.3 17.5 %scatter_custom_fusion.2 = f32[3,2304]{0,1:T(8,128)S(1)} fusion(s32[3072]{0:T(1024)S(1)} %reshape.153, f32[3072,3]{1,0:T(8,128)} %copy.266, f32[]{:T(128)} %constant.47.clone.1), kind=kCustom, calls=%fused_computation.105 | custom fusion | flops 9216 | bytes 28160 | tf_op jit(solution)/shard_map/transpose(jvp())/scatter-add | solution.py:57
  (348 shorter events, 224.6 us)
Async XLA Ops:
  7.2 158.8 %copy-start = (f32[128,128]{1,0:T(8,128)S(1)}, f32[128,128]{1,0:T(8,128)}, u32[]{:S(2)}) copy-start(f32[128,128]{1,0:T(8,128)} %param.23) | copy-start | bytes 196612
  7.2 419.1 %all-reduce.3.cloned.1.call-start = ((), (), s32[]{:S(2)}) async-start(), calls=%async_computation | async-start | bytes 4194304 | tf_op jit(solution)/shard_map/psum | solution.py:271
  8.6 7.5 %collective-permute-start.1 = (f32[1,1,4,256]{3,1,2,0:T(1,128)S(1)}, f32[1,1,4,256]{3,1,2,0:T(1,128)S(1)}, u32[]{:S(2)}, u32[]{:S(2)}) collective-permute-start(f32[1,1,4,256]{3,1,2,0:T(1,128)S(1)} %pad_maximum_fusion.5), channel_id=1, source_target_pairs={{16,0},{32,16},{48,32},{64,48},{80,64},{96,80},{112,96},{128,112},... | collective-permute-start | bytes 12296 | tf_op jit(solution)/shard_map/ppermute | solution.py:31
  9.3 6.8 %collective-permute-start = (f32[1,1,4,256]{3,1,2,0:T(1,128)S(1)}, f32[1,1,4,256]{3,1,2,0:T(1,128)S(1)}, u32[]{:S(2)}, u32[]{:S(2)}) collective-permute-start(f32[1,1,4,256]{3,1,2,0:T(1,128)S(1)} %pad_maximum_fusion.5), channel_id=1, source_target_pairs={{0,16},{16,32},{32,48},{48,64},{64,80},{80,96},{96,112},{112,128},... | collective-permute-start | bytes 12296 | tf_op jit(solution)/shard_map/ppermute | solution.py:28
  16.8 6.3 collective-permute-start.3
  17.3 5.8 collective-permute-start.2
  62.2 15.3 %copy-start.17 = (f32[256,128]{1,0:T(8,128)}, f32[256,128]{1,0:T(8,128)S(1)}, u32[]{:S(2)}) copy-start(f32[256,128]{1,0:T(8,128)S(1)} %convolution_add_fusion.5) | copy-start | bytes 393220
  62.3 4.9 collective-permute-start.5
  62.3 4.9 collective-permute-start.4
  67.2 10.2 %collective-permute-start.7 = (bf16[3,1,256,128]{3,2,1,0:T(8,128)(2,1)S(1)}, bf16[3,1,256,128]{3,2,1,0:T(8,128)(2,1)S(1)}, u32[]{:S(2)}, u32[]{:S(2)}) collective-permute-start(bf16[3,1,256,128]{3,2,1,0:T(8,128)(2,1)S(1)} %pad_maximum_fusion.1), channel_id=1, source_target_pairs={{1,0},{2,1},{3,2},{4,3},{5,4},{6,5},{7,6},{8,7},{9,8},{10,9},{11,1... | collective-permute-start | bytes 589832 | tf_op jit(solution)/shard_map/ppermute | solution.py:31
  67.3 10.1 %collective-permute-start.6 = (bf16[3,1,256,128]{3,2,1,0:T(8,128)(2,1)S(1)}, bf16[3,1,256,128]{3,2,1,0:T(8,128)(2,1)S(1)}, u32[]{:S(2)}, u32[]{:S(2)}) collective-permute-start(bf16[3,1,256,128]{3,2,1,0:T(8,128)(2,1)S(1)} %pad_maximum_fusion.1), channel_id=1, source_target_pairs={{0,1},{1,2},{2,3},{3,4},{4,5},{5,6},{6,7},{7,8},{8,9},{9,10},{10,1... | collective-permute-start | bytes 589832 | tf_op jit(solution)/shard_map/ppermute | solution.py:28
  166.3 350.0 %copy-start.52 = (f32[256,128]{1,0:T(8,128)}, f32[256,128]{1,0:T(8,128)S(1)}, u32[]{:S(2)}) copy-start(f32[256,128]{1,0:T(8,128)S(1)} %fusion.196) | copy-start | bytes 393220
  428.5 88.0 %copy-start.50 = (f32[128]{0:T(128)S(1)}, f32[128]{0:T(128)}, u32[]{:S(2)}) copy-start(f32[128]{0:T(128)} %param.24) | copy-start | bytes 1540
  428.5 88.3 %copy-start.21 = (f32[2,2,128,128]{3,2,1,0:T(8,128)S(1)}, f32[2,2,128,128]{3,2,1,0:T(8,128)}, u32[]{:S(2)}) copy-start(f32[2,2,128,128]{3,2,1,0:T(8,128)} %param.22) | copy-start | bytes 786436
  527.2 19.5 %copy-start.51 = (f32[128]{0:T(128)S(1)}, f32[128]{0:T(128)}, u32[]{:S(2)}) copy-start(f32[128]{0:T(128)} %param.24) | copy-start | bytes 1540
  544.6 10.7 %collective-permute-start.8 = (f32[3,256,128]{2,1,0:T(8,128)S(1)}, f32[3,256,128]{2,1,0:T(8,128)S(1)}, u32[]{:S(2)}, u32[]{:S(2)}) collective-permute-start(f32[3,256,128]{2,1,0:T(8,128)S(1)} %get-tuple-element.335), channel_id=1, source_target_pairs={{15,0},{0,1},{1,2},{2,3},{3,4},{4,5},{5,6},{6,7},{7,8},{8,9},{9,10... | collective-permute-start | bytes 1179656 | tf_op jit(solution)/shard_map/ppermute | solution.py:19
  546.7 12.5 %collective-permute-start.9 = (f32[3,256,128]{2,1,0:T(8,128)S(1)}, f32[3,256,128]{2,1,0:T(8,128)S(1)}, u32[]{:S(2)}, u32[]{:S(2)}) collective-permute-start(f32[3,256,128]{2,1,0:T(8,128)S(1)} %get-tuple-element.336), channel_id=1, source_target_pairs={{1,0},{2,1},{3,2},{4,3},{5,4},{6,5},{7,6},{8,7},{9,8},{10,9},{11,1... | collective-permute-start | bytes 1179656 | tf_op jit(solution)/shard_map/ppermute | solution.py:19
  548.4 12.6 %copy-start.15 = (f32[256,12,128]{2,1,0:T(8,128)S(1)}, f32[256,12,128]{2,1,0:T(8,128)}, u32[]{:S(2)}) copy-start(f32[256,12,128]{2,1,0:T(8,128)} %copy-done.14) | copy-start | bytes 4718596
  559.3 5.4 collective-permute-start.10
  561.0 5.6 collective-permute-start.11
  637.7 2.9 collective-permute-start.12
  637.8 5.9 collective-permute-start.13
  643.7 3.1 collective-permute-start.14
  646.1 4.2 collective-permute-start.15
  (46 other events, 215.2 us)
Sparse Core Ops, SparseCore 0:
  164.6 261.6 all-reduce.2
where the time goes:
time: 664 us; the launch traced here: 658 us
  waiting for transfers between devices  280 us (42%)
  matrix products  184 us (28%)
  local copies, waits for them, and re-layouts  78.6 us (12%)
  other arithmetic  68.8 us (10%)
  starting transfers between devices  24.2 us (4%)
  between operations  15.2 us (2%)
    psum x1, waiting for transfers between devices, per_device(): structure = lax.psum(partial_sf, ('gx', 'gy'))  260 us
    scatter-add x2, other arithmetic, interact(): relative = src_pos[:, neighbour_ids] - own_pos[:, :, None]  34.7 us
    dot_general x6, matrix products, interact(): jnp.einsum('anc,xan->xac', weight_one * source, unit_vec, precision=highest)  27.5 us
    gather x4, local copies, waits for them, and re-layouts, interact(): source = h_src[neighbour_ids]  24.7 us
    dot_general x4, matrix products, interact(): jnp.einsum('anr,rc->anc', radial_basis, radial_pair[1], precision=highest)  18.9 us
    dot_general x8, matrix products, structure_term(): imag_part = lax.dot_general(sine_part, charges, dims, precision=highest)  18.9 us
    dot_general x8, matrix products, fold_terms(): jnp.dot(sine_part, weight_im, precision=highest)  18.7 us
    dot_general x8, matrix products, structure_term(): real_part = lax.dot_general(cosine, charges, dims, precision=highest)  18.7 us
  transfers between devices with their start and end apart: 17, of which 8 were waited for; matrix products, arithmetic and copies ran while one was open for 3% of the time, Pallas kernels for 0%

commit v1 on v0

--- a/solution.py
+++ b/solution.py
@@ -268,7 +268,7 @@
         )
 
     partial_sf = lax.map(term_block, jnp.arange(block_total)).reshape(wave_count, 2 * lat_width)
-    structure = lax.psum(partial_sf, ("gx", "gy"))
+    structure = lax.psum(lax.psum(partial_sf, "gy"), "gx")
     weighted = green_weight[:, None] * structure
 
     def fold_block(block_idx, carried):

time: 664 us -> 620 us (0.934)
  waiting for transfers between devices: 280 us -> 238 us
    psum x1 -> x2, waiting for transfers between devices: 260 us -> 217 us  [per_device(): structure = lax.psum(lax.psum(partial_sf, 'gy'), 'gx')]
  transfers between devices with their start and end apart: 17 -> 18, of which waited for: 8 -> 9; matrix products, arithmetic and copies ran while one was open for 3% -> 3% of each run, Pallas kernels for 0% -> 0%
where the time goes in v1:
time: 620 us; the launch traced here: 613 us
  waiting for transfers between devices  238 us (38%)
  matrix products  184 us (30%)
  local copies, waits for them, and re-layouts  78 us (13%)
  other arithmetic  68.7 us (11%)
  starting transfers between devices  22.8 us (4%)
  between operations  15.3 us (2%)
  loops' own time  6.43 us (1%)
    psum x2, waiting for transfers between devices, per_device(): structure = lax.psum(lax.psum(partial_sf, 'gy'), 'gx')  217 us
    scatter-add x2, other arithmetic, interact(): relative = src_pos[:, neighbour_ids] - own_pos[:, :, None]  34.7 us
    dot_general x6, matrix products, interact(): jnp.einsum('anc,xan->xac', weight_one * source, unit_vec, precision=highest)  27.5 us
    gather x4, local copies, waits for them, and re-layouts, interact(): source = h_src[neighbour_ids]  24.7 us
    dot_general x8, matrix products, structure_term(): imag_part = lax.dot_general(sine_part, charges, dims, precision=highest)  18.8 us
    dot_general x4, matrix products, interact(): jnp.einsum('anr,rc->anc', radial_basis, radial_pair[1], precision=highest)  18.8 us
    dot_general x8, matrix products, fold_terms(): jnp.dot(sine_part, weight_im, precision=highest)  18.7 us
    dot_general x8, matrix products, structure_term(): real_part = lax.dot_general(cosine, charges, dims, precision=highest)  18.7 us
  transfers between devices with their start and end apart: 18, of which 9 were waited for; matrix products, arithmetic and copies ran while one was open for 3% of the time, Pallas kernels for 0%

profile of v1, /device:TPU:127, one launch (start us, length us, event | category | flops | bytes accessed | tf_op | source)
XLA Modules:
  0.0 613.3 jit_solution(6820723377399730641)
XLA Ops:
  17.3 4.3 collective-permute-start.2
  24.4 8.1 %gather_fusion = f32[3072,3]{1,0:T(8,128)S(1)} fusion(f32[3,2304]{0,1:T(8,128)S(1)} %bitcast.271, s32[3072]{0:T(1024)S(1)} %broadcast_clamp_fusion), kind=kCustom, calls=%fused_computation | custom fusion | bytes 86016 | tf_op jit(solution)/shard_map/jvp()/gather | solution.py:57
  36.6 10.8 %gather_fusion.1 = f32[3072,128]{1,0:T(8,128)} fusion(f32[2304,128]{1,0:T(8,128)S(1)} %fusion.133, s32[3072]{0:T(1024)S(1)} %broadcast_clamp_fusion), kind=kCustom, calls=%fused_computation.1 | custom fusion | bytes 3158016 | tf_op jit(solution)/shard_map/jvp()/gather | solution.py:72
  49.1 4.2 multiply_reduce_fusion.1
  53.3 4.4 multiply_multiply_fusion
  58.0 4.0 multiply_reduce_fusion.3
  67.3 5.2 collective-permute-start.6
  72.5 5.0 convolution_multiply_fusion.1
  77.8 10.8 %gather_fusion.2 = f32[3072,128]{1,0:T(8,128)} fusion(f32[2304,128]{1,0:T(8,128)S(1)} %bitcast_convert_fusion, s32[3072]{0:T(1024)S(1)} %broadcast_clamp_fusion), kind=kCustom, calls=%fused_computation.2 | custom fusion | bytes 3158016 | tf_op jit(solution)/shard_map/jvp()/gather | solution.py:72
  90.1 6.9 %copy_multiply_fusion.1 = (f32[256,12,128]{2,0,1:T(8,128)S(1)}, f32[256,128]{1,0:T(8,128)S(1)}, f32[256,12,128]{2,0,1:T(8,128)}) fusion(f32[256,12,128]{2,1,0:T(8,128)S(1)} %reshape.168, f32[256,12,128]{2,0,1:T(8,128)} %convolution_multiply_fusion.1, f32[256,12]{0,1:T(8,128)S(1)} %fusion.161, f32[2,2,8,128]{3,2,1,0:T(8,128)} %param.21, ...), kind=kOutput, calls=%fused_computation.121 | convolution fusion | flops 39337984 | bytes 6451232 | tf_op jit(solution)/shard_map/jvp(anr,rc->anc)/dot_general | solution.py:69
  97.3 3.9 multiply_reduce_fusion.2
  102.4 62.0 %while.26 = (s32[]{:T(128)}, f32[8,512,128]{2,1,0:T(8,128)}, f32[3,256]{1,0:T(4,128)S(1)}, s32[8]{0:T(128)S(1)}, f32[3,4096]{1,0:T(4,128)}, /*index=5*/f32[256,6...) while((s32[]{:T(128)}, f32[8,512,128]{2,1,0:T(8,128)}, ...), condition=%wide.region_7.8_spmd, body=%wide.region_6.7_spmd.sunk | while | flops 202702848 | bytes 2003167 | solution.py:270
  164.5 98.4 %all-reduce.4.cloned.1.call-done = f32[4096,128]{1,0:T(8,128)} async-done(((f32[4096,128]{1,0:T(8,128)}), f32[4096,128]{1,0:T(8,128)}) %all-reduce.4.cloned.1.call-update) | async-done | bytes 2097168 | tf_op jit(solution)/shard_map/psum | solution.py:271
  264.1 119.0 %all-reduce.6.cloned.1.call-done = f32[4096,128]{1,0:T(8,128)} async-done(((f32[4096,128]{1,0:T(8,128)}), f32[4096,128]{1,0:T(8,128)}) %all-reduce.6.cloned.1.call-update) | async-done | bytes 2097168 | tf_op jit(solution)/shard_map/psum | solution.py:271
  385.3 87.4 %while.27 = (s32[]{:T(128)}, f32[256,64]{0,1:T(8,128)S(1)}, f32[3,256]{1,0:T(4,128)S(1)}, f32[3,256]{1,0:T(4,128)S(1)}, f32[3,4096]{1,0:T(4,128)}, /*index=5*/f3...) while((s32[]{:T(128)}, f32[256,64]{0,1:T(8,128)S(1)}, ...), condition=%wide.region_11.12_spmd.clone, body=%wide.region_10.11_spmd.clone.sunk | while | flops 410437120 | bytes 3739922 | solution.py:280
  474.8 4.0 fusion.88
  484.2 17.4 %scatter_fusion = f32[2304,128]{1,0:T(8,128)S(1)} fusion(f32[2304,128]{1,0:T(8,128)S(1)} %pad.3, s32[3072]{0:T(1024)S(1)} %reshape.153, f32[3072,128]{1,0:T(8,128)S(1)} %reshape.179), kind=kCustom, calls=%fused_computation.3 | custom fusion | flops 393216 | bytes 4730880 | tf_op jit(solution)/shard_map/transpose(jvp())/scatter-add | solution.py:72
  507.1 5.7 collective-permute-done.8
  523.2 4.1 fusion.47
  527.4 5.3 fusion.89
  532.7 6.2 %fusion.80 = (f32[256,12]{1,0:T(8,128)}, f32[256,12]{1,0:T(8,128)}, f32[256,3,12]{2,1,0:T(4,128)}) fusion(f32[256,12]{1,0:T(8,128)S(1)} %copy-done.30, f32[3,256]{0,1:T(8,128)S(1)} %copy.230, f32[256,12,3]{1,0,2:T(8,128)S(1)} %copy-done.13, f32[256,3,12]{2,1,0:T(4,128)S(1)} %fusion.47, f32[256,12,128]{2,0,1:T(8,128)S(1)} %copy-done.7, ...), kind=kOutput, calls=%fused_computation.110 | convolution fusion | flops 14509056 | bytes 2247680 | tf_op jit(solution)/shard_map/transpose(jvp(anc,xan->xac))/dot_general | solution.py:76
  542.1 3.9 fusion.52
  553.6 17.2 %scatter_custom_fusion.1 = f32[3,2304]{0,1:T(8,128)S(1)} fusion(s32[3072]{0:T(1024)S(1)} %reshape.153, f32[3072,3]{1,0:T(8,128)S(1)} %copy.264, f32[]{:T(128)} %constant.47.clone.1), kind=kCustom, calls=%fused_computation.107 | custom fusion | flops 9216 | bytes 27652 | tf_op jit(solution)/shard_map/transpose(jvp())/scatter-add | solution.py:57
  572.5 17.5 %scatter_custom_fusion.2 = f32[3,2304]{0,1:T(8,128)S(1)} fusion(s32[3072]{0:T(1024)S(1)} %reshape.153, f32[3072,3]{1,0:T(8,128)} %copy.266, f32[]{:T(128)} %constant.47.clone.1), kind=kCustom, calls=%fused_computation.105 | custom fusion | flops 9216 | bytes 28160 | tf_op jit(solution)/shard_map/transpose(jvp())/scatter-add | solution.py:57
  (351 shorter events, 225.3 us)
Async XLA Ops:
  7.2 256.6 %copy-start = (f32[128,128]{1,0:T(8,128)S(1)}, f32[128,128]{1,0:T(8,128)}, u32[]{:S(2)}) copy-start(f32[128,128]{1,0:T(8,128)} %param.23) | copy-start | bytes 196612
  7.2 255.8 %all-reduce.4.cloned.1.call-start = ((), (), s32[]{:S(2)}) async-start(), calls=%async_computation | async-start | bytes 4194304 | tf_op jit(solution)/shard_map/psum | solution.py:271
  8.6 7.5 %collective-permute-start.1 = (f32[1,1,4,256]{3,1,2,0:T(1,128)S(1)}, f32[1,1,4,256]{3,1,2,0:T(1,128)S(1)}, u32[]{:S(2)}, u32[]{:S(2)}) collective-permute-start(f32[1,1,4,256]{3,1,2,0:T(1,128)S(1)} %pad_maximum_fusion.5), channel_id=1, source_target_pairs={{16,0},{32,16},{48,32},{64,48},{80,64},{96,80},{112,96},{128,112},... | collective-permute-start | bytes 12296 | tf_op jit(solution)/shard_map/ppermute | solution.py:31
  9.3 6.8 %collective-permute-start = (f32[1,1,4,256]{3,1,2,0:T(1,128)S(1)}, f32[1,1,4,256]{3,1,2,0:T(1,128)S(1)}, u32[]{:S(2)}, u32[]{:S(2)}) collective-permute-start(f32[1,1,4,256]{3,1,2,0:T(1,128)S(1)} %pad_maximum_fusion.5), channel_id=1, source_target_pairs={{0,16},{16,32},{32,48},{48,64},{64,80},{80,96},{96,112},{112,128},... | collective-permute-start | bytes 12296 | tf_op jit(solution)/shard_map/ppermute | solution.py:28
  16.8 6.3 %collective-permute-start.3 = (f32[3,1,4,256]{3,1,2,0:T(1,128)S(1)}, f32[3,1,4,256]{3,1,2,0:T(1,128)S(1)}, u32[]{:S(2)}, u32[]{:S(2)}) collective-permute-start(f32[3,1,4,256]{3,1,2,0:T(1,128)S(1)} %pad_maximum_fusion.4), channel_id=1, source_target_pairs={{1,0},{2,1},{3,2},{4,3},{5,4},{6,5},{7,6},{8,7},{9,8},{10,9},{11,1... | collective-permute-start | bytes 36872 | tf_op jit(solution)/shard_map/ppermute | solution.py:31
  17.3 5.8 collective-permute-start.2
  62.3 4.9 collective-permute-start.5
  62.3 4.9 collective-permute-start.4
  67.2 10.3 %collective-permute-start.7 = (bf16[3,1,256,128]{3,2,1,0:T(8,128)(2,1)S(1)}, bf16[3,1,256,128]{3,2,1,0:T(8,128)(2,1)S(1)}, u32[]{:S(2)}, u32[]{:S(2)}) collective-permute-start(bf16[3,1,256,128]{3,2,1,0:T(8,128)(2,1)S(1)} %pad_maximum_fusion.1), channel_id=1, source_target_pairs={{1,0},{2,1},{3,2},{4,3},{5,4},{6,5},{7,6},{8,7},{9,8},{10,9},{11,1... | collective-permute-start | bytes 589832 | tf_op jit(solution)/shard_map/ppermute | solution.py:31
  67.3 10.2 %collective-permute-start.6 = (bf16[3,1,256,128]{3,2,1,0:T(8,128)(2,1)S(1)}, bf16[3,1,256,128]{3,2,1,0:T(8,128)(2,1)S(1)}, u32[]{:S(2)}, u32[]{:S(2)}) collective-permute-start(bf16[3,1,256,128]{3,2,1,0:T(8,128)(2,1)S(1)} %pad_maximum_fusion.1), channel_id=1, source_target_pairs={{0,1},{1,2},{2,3},{3,4},{4,5},{5,6},{6,7},{7,8},{8,9},{9,10},{10,1... | collective-permute-start | bytes 589832 | tf_op jit(solution)/shard_map/ppermute | solution.py:28
  164.4 98.6 %copy-start.44 = (f32[4096]{0:T(1024)S(1)}, f32[4096]{0:T(1024)}, u32[]{:S(2)}) copy-start(f32[4096]{0:T(1024)} %get-tuple-element.319) | copy-start | bytes 49156
  164.4 98.6 %copy-start.41 = (f32[256,12]{0,1:T(8,128)S(1)}, f32[256,12]{0,1:T(8,128)}, u32[]{:S(2)}) copy-start(f32[256,12]{0,1:T(8,128)} %get-tuple-element.345) | copy-start | bytes 36868
  164.4 218.6 %all-reduce.6.cloned.1.call-start = ((), (), s32[]{:S(2)}) async-start(), calls=%async_computation.1 | async-start | bytes 4194304 | tf_op jit(solution)/shard_map/psum | solution.py:271
  264.1 209.0 %copy-start.52 = (f32[256,128]{1,0:T(8,128)}, f32[256,128]{1,0:T(8,128)S(1)}, u32[]{:S(2)}) copy-start(f32[256,128]{1,0:T(8,128)S(1)} %fusion.196) | copy-start | bytes 393220
  385.3 88.0 %copy-start.50 = (f32[128]{0:T(128)S(1)}, f32[128]{0:T(128)}, u32[]{:S(2)}) copy-start(f32[128]{0:T(128)} %param.24) | copy-start | bytes 1540
  385.3 88.3 %copy-start.21 = (f32[2,2,128,128]{3,2,1,0:T(8,128)S(1)}, f32[2,2,128,128]{3,2,1,0:T(8,128)}, u32[]{:S(2)}) copy-start(f32[2,2,128,128]{3,2,1,0:T(8,128)} %param.22) | copy-start | bytes 786436
  501.6 11.2 %collective-permute-start.8 = (f32[3,256,128]{2,1,0:T(8,128)S(1)}, f32[3,256,128]{2,1,0:T(8,128)S(1)}, u32[]{:S(2)}, u32[]{:S(2)}) collective-permute-start(f32[3,256,128]{2,1,0:T(8,128)S(1)} %get-tuple-element.335), channel_id=1, source_target_pairs={{15,0},{0,1},{1,2},{2,3},{3,4},{4,5},{5,6},{6,7},{7,8},{8,9},{9,10... | collective-permute-start | bytes 1179656 | tf_op jit(solution)/shard_map/ppermute | solution.py:19
  501.9 14.2 %collective-permute-start.9 = (f32[3,256,128]{2,1,0:T(8,128)S(1)}, f32[3,256,128]{2,1,0:T(8,128)S(1)}, u32[]{:S(2)}, u32[]{:S(2)}) collective-permute-start(f32[3,256,128]{2,1,0:T(8,128)S(1)} %get-tuple-element.336), channel_id=1, source_target_pairs={{1,0},{2,1},{3,2},{4,3},{5,4},{6,5},{7,6},{8,7},{9,8},{10,9},{11,1... | collective-permute-start | bytes 1179656 | tf_op jit(solution)/shard_map/ppermute | solution.py:19
  516.2 4.4 collective-permute-start.10
  516.3 5.6 collective-permute-start.11
  592.9 2.6 collective-permute-start.12
  593.1 5.9 collective-permute-start.13
  599.0 3.2 collective-permute-start.14
  601.4 4.2 collective-permute-start.15
  (47 other events, 259.3 us)
Sparse Core Ops, SparseCore 0:
  164.5 98.3 all-reduce.3
  265.4 117.6 all-reduce.5
